TPU v7x, 32 devices: a whole 2x2x4 slice. The times are simulated.
32 devices in a mesh: circ: 8 (over z, core), span: 4 (over y, x).
Axes of the slice: x: 2, y: 2, z: 4, core: 2. Of those that a mesh axis runs over, the one named last changes fastest.
Arguments:
- adjoint_rotor: float32 [6, 8, 4, 2048], P(None, 'span', None, 'circ'), may hold values from -6 to 6
- adjoint_stator: float32 [6, 8, 4, 2048], P(None, 'span', None, 'circ'), may hold values from -6 to 6
- jac_diag_rotor: float32 [6, 8, 4, 2048], P(None, 'span', None, 'circ'), may hold values from 2 to 4
- jac_diag_stator: float32 [6, 8, 4, 2048], P(None, 'span', None, 'circ'), may hold values from 2 to 4
- jac_off_rotor: bfloat16 [6, 6, 8, 4, 2048], P(None, None, 'span', None, 'circ'), may hold values from -1 to 1
- jac_off_stator: bfloat16 [6, 6, 8, 4, 2048], P(None, None, 'span', None, 'circ'), may hold values from -1 to 1
- source_rotor: float32 [6, 8, 4, 2048], P(None, 'span', None, 'circ'), may hold values from -6 to 6
- source_stator: float32 [6, 8, 4, 2048], P(None, 'span', None, 'circ'), may hold values from -6 to 6
- rotor_state: bfloat16 [6, 8, 2048], P(None, 'span', 'circ'), may hold values from -6 to 6
- margin_block: int32 [8, 16, 4], P('span'), may hold values from 0 to 15, as said below
- face_count: int32 [8, 16], P('span'), may hold values from 1 to 4
- margin_weight: float32 [8, 16, 4, 128], P('span'), may hold values from 0.2 to 1
Outputs:
- rotor_adjoint: float32 [6, 8, 4, 2048], P(None, 'span', None, 'circ')
- stator_adjoint: float32 [6, 8, 4, 2048], P(None, 'span', None, 'circ')
Inputs may be any that keep to these rules, and one draw needn't show every extreme that they name: `margin_block`: entry k of the list of stator block b in spanwise row s is rotor block (b + o + 2 * 2 * s + 1 + j + k) mod 16, with one o for the whole array and j from 0 to 2 for each block of each row.
All inputs are finite; a program needn't handle non-finite values.
Results may differ from a plain program's by a relative error of at most 0.00055.
Values may be sent and summed in bfloat16 or wider, within the bound.
No kernel may reach another device: no remote copies, remote signals or barrier semaphores. Data moves between devices by JAX's collectives and lax.ppermute only.
A program may use at most 64 MiB of HBM per device.

v0:
```python
import jax
import jax.numpy as jnp
from jax import lax
from jax.experimental import pallas as pl
from jax.experimental.pallas import tpu as pltpu
from jax.sharding import PartitionSpec as P

step_size = 0.1
coupling = 0.2
carry = step_size * coupling
REACH = 8
TILE = 128
f32 = jnp.float32
params = pltpu.CompilerParams(vmem_limit_bytes=24 * 1024 * 1024)


def iota(shape, dim):
    return lax.broadcasted_iota(jnp.int32, shape, dim)


def wrapped(x, count):
    if count & (count - 1) == 0:
        return jnp.bitwise_and(x, count - 1)
    return lax.rem(x + 4 * count, count)


def lanes_apart(x):
    cells = x.shape[1]
    lane = iota(x.shape, 1)
    before = jnp.where(lane == 0, 0.0, pltpu.roll(x, 1, 1))
    after = jnp.where(lane == cells - 1, 0.0, pltpu.roll(x, cells - 1, 1))
    return before + after


def layers_apart(x):
    return pltpu.roll(x, 1, 0) + pltpu.roll(x, 7, 0)


def edge_pick(row, cells):
    at = iota((8, cells), 0)
    lane = iota((8, cells), 1)
    first = jnp.logical_and(at == row, lane == 0)
    last = jnp.logical_and(at == 4 + row, lane == cells - 1)
    return jnp.where(jnp.logical_or(first, last), 1.0, 0.0).astype(f32)


def flux_of(primal, adjoint):
    speeds = jnp.sqrt(1.0 + primal * primal)
    over = jnp.sum(primal * adjoint, axis=0, keepdims=True)
    under = 6.0 + jnp.sum(primal * primal, axis=0, keepdims=True)
    return speeds * adjoint + 0.5 * primal * (over / under)


def jacobian_row(diag, off, state, v, s, var_count):
    total = diag[v, s] * state[v]
    for w in range(var_count):
        total = total + off[w, v, s].astype(f32) * state[w]
    return total


def pull_row(flux, weights, margin, count, s, slot, first_block, base, total):
    target = wrapped(first_block + slot + total, total)
    acc = jnp.zeros((8, TILE), f32)
    for e in range(REACH):
        b = wrapped(base + slot + e, total)
        k = wrapped(target - margin[s, 0, b] + total, total)
        live = jnp.where(k < count[s, b], 1.0, 0.0).astype(f32)
        kept = jnp.minimum(k, weights.shape[2] - 1)
        acc = acc + (weights[s, b, pl.ds(kept, 1), :] * live) * flux(slot + e)
    return acc


def first_kernel(*refs):
    outer, refs = refs[:12], refs[12:]
    v_r, v_s, out, a_r, a_s, weights, margin, count = refs[:8]
    jd_r, jd_s, jo_r, jo_s, src_r, src_s, state = refs[8:15]
    xs, sems = refs[15:19], refs[19]
    var_count, rows, layers, cells = a_r.shape
    own_blocks = cells // TILE
    inner = (a_r, a_s, jd_r, jd_s, jo_r, jo_s, src_r, src_s, state, margin, count, weights)
    copies = [pltpu.make_async_copy(x, y, sems.at[n]) for n, (x, y) in enumerate(zip(outer, inner))]
    for copy in copies:
        copy.start()
    out[...] = jnp.zeros(out.shape, f32)
    for x in xs:
        x[...] = jnp.zeros(x.shape, f32)
    for copy in copies:
        copy.wait()
    fields = ((a_r, jd_r, jo_r, src_r, v_r, xs[0], xs[2]), (a_s, jd_s, jo_s, src_s, v_s, xs[1], xs[3]))
    for a, jd, jo, src, partial, x_a, x_p in fields:
        for v in range(var_count):
            for s in range(rows):
                x_a[v * rows + s, 0:layers, :] = a[v, s]
        for s in range(rows):
            state_row = [a[v, s] for v in range(var_count)]
            for v in range(var_count):
                wide = x_a[v * rows + s]
                beside = (lanes_apart(wide) + layers_apart(wide))[0:layers]
                if s > 0:
                    beside = beside + a[v, s - 1]
                if s < rows - 1:
                    beside = beside + a[v, s + 1]
                res = jacobian_row(jd, jo, state_row, v, s, var_count) - coupling * beside - src[v, s]
                new = state_row[v] - step_size * res
                partial[v, s] = new
                x_p[v * rows + s, 0:layers, :] = new
    edges = jnp.zeros((8, TILE), f32)
    for q in range(4):
        flat = xs[q][...].reshape(TILE, cells)
        edges = edges + lax.dot_general(
            edge_pick(q, cells), flat, (((1,), (1,)), ((), ())), preferred_element_type=f32
        )
    for v in range(var_count):
        rotor = state[v].astype(f32)
        for s in range(rows):
            for i in range(own_blocks):
                cut = slice(i * TILE, (i + 1) * TILE)
                at = s * 8 + v
                out[i, at : at + 1, :] = rotor[s : s + 1, cut]
                out[i, rows * 8 + at : rows * 8 + at + 1, :] = a_s[v, s, 0:1, cut]
                out[i, rows * 16 + at : rows * 16 + at + 1, :] = v_s[v, s, 0:1, cut]
    for side, i in ((0, 0), (1, own_blocks - 1)):
        out[i, 6:8, :] = edges[4 * side : 4 * side + 2]
        out[i, 14:16, :] = edges[4 * side + 2 : 4 * side + 4]


def second_kernel(
    g, v_r, v_s, a_r, a_s, weights, margin, count,
    o_r, o_s, h_r, h_s, q_out, p_out, up, down, flux, held, spot,
):
    var_count, rows, layers, cells = a_r.shape
    total = g.shape[0]
    own_blocks = cells // TILE
    entries = weights.shape[2]
    spread = REACH + own_blocks + 1
    first_block = lax.axis_index("circ") * own_blocks
    row8 = iota((8, TILE), 0)
    lane = iota((8, TILE), 1)
    lane_all = iota((layers, cells), 1)
    layer_all = iota((layers, cells), 0)
    edge = jnp.logical_or(lane_all == 0, lane_all == cells - 1)
    left = wrapped(first_block - 1 + total, total)
    right = wrapped(first_block + own_blocks, total)

    spot[0:2, :] = g[left, 6:8, :]
    spot[2:4, :] = g[left, 14:16, :]
    spot[4:6, :] = g[right, 6:8, :]
    spot[6:8, :] = g[right, 14:16, :]
    spots = spot[...]
    columns = [
        lax.dot_general(spots, edge_pick(q, cells), (((0,), (0,)), ((), ())), preferred_element_type=f32)
        for q in range(4)
    ]

    def block(s, b):
        primal = jnp.zeros((8, TILE), f32)
        for k in range(entries):
            live = jnp.where(k < count[s, b], 1.0, 0.0).astype(f32)
            primal = primal + (weights[s, b, k : k + 1, :] * live) * g[margin[s, k, b], s * 8 : s * 8 + 8, :]
        primal = jnp.where(row8 < var_count, primal, 0.0)
        adjoint = g[b, rows * 8 + s * 8 : rows * 8 + s * 8 + 8, :]
        return primal, flux_of(primal, adjoint)

    def advanced(s, b, moved):
        at = slice(rows * 8 + s * 8, rows * 8 + s * 8 + 8)
        place = lax.rem(b, own_blocks)
        before = jnp.where(place == 0, carry, 0.0).astype(f32)
        after = jnp.where(place == own_blocks - 1, carry, 0.0).astype(f32)
        low = pltpu.roll(g[wrapped(b - 1 + total, total), at, :], 1, 1)
        high = pltpu.roll(g[wrapped(b + 1, total), at, :], TILE - 1, 1)
        base = g[b, rows * 16 + s * 8 : rows * 16 + s * 8 + 8, :]
        base = base + jnp.where(lane == 0, low * before, 0.0) + jnp.where(lane == TILE - 1, high * after, 0.0)
        return base - step_size * moved

    for s in range(rows):
        base = first_block - margin[s, 0, 0] - 5 + 4 * total
        for t in range(spread):
            b = wrapped(base - 1 + t, total)
            primal, moved = block(s, b)
            flux[s, t] = moved.astype(jnp.bfloat16).astype(f32)
            if 0 < t < spread - 1:
                q_out[s, t - 1] = primal
                p_out[s, t - 1] = advanced(s, b, moved)
        own = []
        for i in range(own_blocks):
            primal, moved = block(s, first_block + i)
            own.append(moved)
            q_out[s, spread - 2 + i] = primal
            p_out[s, spread - 2 + i] = advanced(s, first_block + i, moved)
        blank = [jnp.zeros((8, TILE), f32)] * (own_blocks - 2)
        side_flux = [block(s, left)[1], block(s, right)[1]]
        pulls = [
            pull_row(lambda t: flux[s, t + 1], weights, margin, count, s, slot, first_block, base, total)
            for slot in range(-1, own_blocks + 1)
        ]

        def at_sides(low, high):
            return jnp.concatenate([pltpu.roll(low, 1, 1), *blank, pltpu.roll(high, TILE - 1, 1)], axis=1)

        pulled = step_size * jnp.concatenate(pulls[1:-1], axis=1)
        pulled_side = step_size * at_sides(pulls[0], pulls[-1])
        pushed = step_size * jnp.concatenate(own, axis=1)
        pushed_side = step_size * at_sides(*side_flux)
        for v in range(var_count):
            at = (v * rows + s) * 8
            cut = slice(at, at + layers)
            o_r[v, s] = (
                v_r[v, s] + carry * columns[0][cut] + jnp.where(layer_all == layers - 1, pulled[v : v + 1], 0.0)
            )
            o_s[v, s] = v_s[v, s] + carry * columns[1][cut] - jnp.where(layer_all == 0, pushed[v : v + 1], 0.0)
            h_r[v, s] = columns[2][cut] + jnp.where(
                edge, carry * a_r[v, s] + jnp.where(layer_all == layers - 1, pulled_side[v : v + 1], 0.0), 0.0
            )
            h_s[v, s] = columns[3][cut] + jnp.where(
                edge, carry * a_s[v, s] - jnp.where(layer_all == 0, pushed_side[v : v + 1], 0.0), 0.0
            )

    last = jnp.concatenate([spots, jnp.ones((8, TILE), f32)], axis=0).astype(jnp.bfloat16)
    for to, s in ((up, rows - 1), (down, 0)):
        at = slice(rows * 8 + s * 8, rows * 8 + s * 8 + 8)
        for j in range(total // 2):
            to[j] = jnp.concatenate([g[2 * j, at, :], g[2 * j + 1, at, :]], axis=0).astype(jnp.bfloat16)
        for v in range(var_count):
            for n, ref in enumerate((a_r, a_s, o_r, o_s)):
                held[v, n * layers : (n + 1) * layers, :] = ref[v, s]
            for i in range(own_blocks):
                to[total // 2 + v * own_blocks + i] = held[v, :, i * TILE : (i + 1) * TILE].astype(jnp.bfloat16)
        to[total // 2 + var_count * own_blocks] = last


def third_kernel(
    low, high, o_r, o_s, h_r, h_s, q, p, a_r, a_s, jd_r, jd_s, jo_r, jo_s, src_r, src_s, weights, margin, count,
    out_r, out_s, flux, x_r, x_s, rows_low, rows_high,
):
    var_count, rows, layers, cells = a_r.shape
    total = weights.shape[1]
    own_blocks = cells // TILE
    spread = REACH + own_blocks + 1
    first_block = lax.axis_index("circ") * own_blocks
    lane = iota((8, TILE), 1)
    layer_all = iota((layers, cells), 0)
    end = total // 2 + var_count * own_blocks
    for x in (x_r, x_s):
        x[...] = jnp.zeros(x.shape, f32)
    for ref, to in ((low, rows_low), (high, rows_high)):
        for v in range(var_count):
            for i in range(own_blocks):
                to[v, :, i * TILE : (i + 1) * TILE] = ref[total // 2 + v * own_blocks + i].astype(f32)
    ends = [ref[end].astype(f32) for ref in (low, high)]
    inside = [jnp.concatenate([x[8:9]] * own_blocks, axis=1) for x in ends]
    group = lax.rem(lax.shift_right_logical(lane, 3), rows)
    corner = jnp.where(group == 0, pltpu.roll(ends[0][0:8], (TILE - 8 * (rows - 1)) % TILE, 1), 0.0)
    corner = corner + jnp.where(group == rows - 1, pltpu.roll(ends[1][0:8], 8 * (rows - 1), 1), 0.0)
    columns = [
        lax.dot_general(corner, edge_pick(n, cells), (((0,), (0,)), ((), ())), preferred_element_type=f32)
        for n in range(2)
    ]

    def halo(ref, b):
        both = ref[lax.shift_right_logical(b, 1)].astype(f32)
        return jnp.where(jnp.bitwise_and(b, 1) == 1, both[8:16], both[0:8])

    extra = []
    for s in range(rows):
        base = first_block - margin[s, 0, 0] - 5 + 4 * total
        own = []
        for t in range(spread - 2 + own_blocks):
            b = wrapped(base + t, total) if t < spread - 2 else first_block + t - (spread - 2)
            adjoint = p[s, t]
            if s == 0:
                adjoint = adjoint + carry * halo(low, b)
            if s == rows - 1:
                adjoint = adjoint + carry * halo(high, b)
            moved = flux_of(q[s, t], adjoint)
            if t < spread - 2:
                flux[s, t] = moved.astype(jnp.bfloat16).astype(f32)
            else:
                own.append(moved)
        pulls = [
            pull_row(lambda t: flux[s, t], weights, margin, count, s, slot, first_block, base, total)
            for slot in range(own_blocks)
        ]
        extra.append((step_size * jnp.concatenate(pulls, axis=1), -step_size * jnp.concatenate(own, axis=1)))

    fields = (
        (o_r, h_r, a_r, jd_r, jo_r, src_r, x_r, out_r, layers - 1),
        (o_s, h_s, a_s, jd_s, jo_s, src_s, x_s, out_s, 0),
    )
    for n, (o, h, a, jd, jo, src, x, out, layer) in enumerate(fields):
        old = slice(n * layers, (n + 1) * layers)
        new = slice((2 + n) * layers, (3 + n) * layers)
        for v in range(var_count):
            for s in range(rows):
                value = o[v, s]
                if s == 0:
                    value = value + carry * rows_low[v, old, :]
                if s == rows - 1:
                    value = value + carry * rows_high[v, old, :]
                x[v * rows + s, 0:layers, :] = value
        for s in range(rows):
            state_row = [x[v * rows + s, 0:layers, :] for v in range(var_count)]
            for v in range(var_count):
                wide = x[v * rows + s]
                beside = (lanes_apart(wide) + layers_apart(wide))[0:layers]
                at = (v * rows + s) * 8
                beside = beside + h[v, s] + carry * columns[n][at : at + layers]
                if s > 0:
                    beside = beside + x[v * rows + s - 1, 0:layers, :]
                else:
                    beside = beside + inside[0] * (rows_low[v, new, :] + carry * a[v, 0])
                if s < rows - 1:
                    beside = beside + x[v * rows + s + 1, 0:layers, :]
                else:
                    beside = beside + inside[1] * (rows_high[v, new, :] + carry * a[v, rows - 1])
                res = jacobian_row(jd, jo, state_row, v, s, var_count) - coupling * beside - src[v, s]
                out[v, s] = (
                    state_row[v] - step_size * res + jnp.where(layer_all == layer, extra[s][n][v : v + 1], 0.0)
                )


def per_device(
    adjoint_rotor,
    adjoint_stator,
    jac_diag_rotor,
    jac_diag_stator,
    jac_off_rotor,
    jac_off_stator,
    source_rotor,
    source_stator,
    rotor_state,
    margin_block,
    face_count,
    margin_weight,
):
    var_count, rows, layers, cells = adjoint_rotor.shape
    own_blocks = cells // TILE
    total = margin_block.shape[1]
    spread = REACH + own_blocks + 1
    field = jax.ShapeDtypeStruct(adjoint_rotor.shape, f32)
    vmem = pl.BlockSpec(memory_space=pltpu.VMEM)
    smem = pl.BlockSpec(memory_space=pltpu.SMEM)
    padded = pltpu.VMEM((TILE // 8, 8, cells), f32)

    margin = jnp.swapaxes(margin_block, 1, 2)
    arguments = (
        adjoint_rotor, adjoint_stator, jac_diag_rotor, jac_diag_stator, jac_off_rotor, jac_off_stator,
        source_rotor, source_stator, rotor_state, margin, face_count, margin_weight,
    )
    shapes = [jax.ShapeDtypeStruct(x.shape, x.dtype) for x in arguments]
    v_r, v_s, share, a_r, a_s, weights, margin, count = pl.pallas_call(
        first_kernel,
        out_shape=(
            field, field, jax.ShapeDtypeStruct((own_blocks, rows * 24, TILE), f32),
            shapes[0], shapes[1], shapes[11], shapes[9], shapes[10],
        ),
        in_specs=[pl.BlockSpec(memory_space=pl.ANY)] * 12,
        out_specs=(vmem,) * 8,
        scratch_shapes=[pltpu.VMEM(x.shape, x.dtype) for x in shapes[2:9]]
        + [padded] * 4
        + [pltpu.SemaphoreType.DMA((12,))],
        compiler_params=params,
        name="local_part",
    )(*arguments)
    whole = lax.all_gather(share, "circ", axis=0, tiled=True)
    tiles = jax.ShapeDtypeStruct((total // 2 + var_count * own_blocks + 1, 16, TILE), jnp.bfloat16)
    listed = jax.ShapeDtypeStruct((rows, spread - 2 + own_blocks, 8, TILE), f32)
    o_r, o_s, h_r, h_s, q, p, up, down = pl.pallas_call(
        second_kernel,
        out_shape=(field, field, field, field, listed, listed, tiles, tiles),
        in_specs=[vmem] * 6 + [smem] * 2,
        out_specs=(vmem,) * 8,
        scratch_shapes=[
            pltpu.VMEM((rows, spread, 8, TILE), f32),
            pltpu.VMEM((var_count, 4 * layers, cells), f32),
            pltpu.VMEM((8, TILE), f32),
        ],
        compiler_params=params,
        name="interface_part",
    )(whole, v_r, v_s, a_r, a_s, weights, margin, count)
    bands = lax.axis_size("span")
    low = lax.ppermute(up, "span", [(i, i + 1) for i in range(bands - 1)])
    high = lax.ppermute(down, "span", [(i + 1, i) for i in range(bands - 1)])
    out_r, out_s = pl.pallas_call(
        third_kernel,
        out_shape=(field, field),
        in_specs=[vmem] * 17 + [smem] * 2,
        out_specs=(vmem,) * 2,
        scratch_shapes=[
            pltpu.VMEM((rows, spread - 2, 8, TILE), f32),
            padded,
            padded,
            pltpu.VMEM((var_count, 4 * layers, cells), f32),
            pltpu.VMEM((var_count, 4 * layers, cells), f32),
        ],
        compiler_params=params,
        name="final_part",
    )(
        low, high, o_r, o_s, h_r, h_s, q, p, a_r, a_s, jac_diag_rotor, jac_diag_stator,
        jac_off_rotor, jac_off_stator, source_rotor, source_stator, weights, margin, count,
    )
    return (out_r, out_s)


def solution(mesh):
    field = P(None, "span", None, "circ")
    placed = (
        (field,) * 4
        + (P(None, None, "span", None, "circ"),) * 2
        + (field,) * 2
        + (P(None, "span", "circ"), P("span", None, None), P("span", None), P("span", None, None, None))
    )
    return jax.shard_map(
        per_device, mesh=mesh, in_specs=placed, out_specs=(field, field), check_vma=False
    )
```

profile of v0, /device:TPU:0, one launch (start us, length us, event | category | flops | bytes accessed | tf_op | source)
XLA Modules:
  0.0 41.0 jit_solution(12197556102859027998)
XLA Ops:
  0.6 0.0 copy-start.15
  0.6 0.7 %copy-done.15 = s32[2,16]{1,0:T(2,128)S(1)} copy-done((s32[2,16]{1,0:T(2,128)S(1)}, s32[2,16]{1,0:T(2,128)}, u32[]{:S(2)}) %copy-start.15) | copy-done | bytes 152
  1.3 0.0 copy-start
  1.3 0.9 %copy-done = bf16[6,6,2,4,256]{4,3,2,1,0:T(4,128)(2,1)S(1)} copy-done((bf16[6,6,2,4,256]{4,3,2,1,0:T(4,128)(2,1)S(1)}, bf16[6,6,2,4,256]{4,3,2,1,0:T(4,128)(2,1)}, u32[]{:S(2)}) %copy-start) | copy-done | bytes 147480
  2.2 0.0 copy-start.2
  2.2 0.9 %copy-done.2 = bf16[6,6,2,4,256]{4,3,2,1,0:T(4,128)(2,1)S(1)} copy-done((bf16[6,6,2,4,256]{4,3,2,1,0:T(4,128)(2,1)S(1)}, bf16[6,6,2,4,256]{4,3,2,1,0:T(4,128)(2,1)}, u32[]{:S(2)}) %copy-start.2) | copy-done | bytes 147480
  3.1 0.0 copy-start.4
  3.1 0.8 %copy-done.4 = f32[6,2,4,256]{3,2,1,0:T(4,128)S(1)} copy-done((f32[6,2,4,256]{3,2,1,0:T(4,128)S(1)}, f32[6,2,4,256]{3,2,1,0:T(4,128)}, u32[]{:S(2)}) %copy-start.4) | copy-done | bytes 49176
  3.9 0.0 copy-start.5
  3.9 0.8 %copy-done.5 = f32[6,2,4,256]{3,2,1,0:T(4,128)S(1)} copy-done((f32[6,2,4,256]{3,2,1,0:T(4,128)S(1)}, f32[6,2,4,256]{3,2,1,0:T(4,128)}, u32[]{:S(2)}) %copy-start.5) | copy-done | bytes 49176
  4.7 0.0 copy-start.6
  4.7 0.8 %copy-done.6 = f32[6,2,4,256]{3,2,1,0:T(4,128)S(1)} copy-done((f32[6,2,4,256]{3,2,1,0:T(4,128)S(1)}, f32[6,2,4,256]{3,2,1,0:T(4,128)}, u32[]{:S(2)}) %copy-start.6) | copy-done | bytes 49176
  5.5 0.0 copy-start.8
  5.5 0.8 %copy-done.8 = f32[6,2,4,256]{3,2,1,0:T(4,128)S(1)} copy-done((f32[6,2,4,256]{3,2,1,0:T(4,128)S(1)}, f32[6,2,4,256]{3,2,1,0:T(4,128)}, u32[]{:S(2)}) %copy-start.8) | copy-done | bytes 49176
  6.3 0.0 copy-start.10
  6.3 0.8 %copy-done.10 = f32[2,16,4,128]{3,2,1,0:T(4,128)S(1)} copy-done((f32[2,16,4,128]{3,2,1,0:T(4,128)S(1)}, f32[2,16,4,128]{3,2,1,0:T(4,128)}, u32[]{:S(2)}) %copy-start.10) | copy-done | bytes 65560
  7.2 0.0 copy-start.11
  7.2 0.8 %copy-done.11 = f32[6,2,4,256]{3,2,1,0:T(4,128)S(1)} copy-done((f32[6,2,4,256]{3,2,1,0:T(4,128)S(1)}, f32[6,2,4,256]{3,2,1,0:T(4,128)}, u32[]{:S(2)}) %copy-start.11) | copy-done | bytes 49176
  8.0 0.0 copy-start.12
  8.0 0.8 %copy-done.12 = f32[6,2,4,256]{3,2,1,0:T(4,128)S(1)} copy-done((f32[6,2,4,256]{3,2,1,0:T(4,128)S(1)}, f32[6,2,4,256]{3,2,1,0:T(4,128)}, u32[]{:S(2)}) %copy-start.12) | copy-done | bytes 49176
  8.8 0.0 copy-start.13
  8.8 0.7 %copy-done.13 = bf16[6,2,256]{2,1,0:T(2,128)(2,1)S(1)} copy-done((bf16[6,2,256]{2,1,0:T(2,128)(2,1)S(1)}, bf16[6,2,256]{2,1,0:T(2,128)(2,1)}, u32[]{:S(2)}) %copy-start.13) | copy-done | bytes 6168
  9.5 0.0 copy-start.14
  9.5 0.7 %copy-done.14 = s32[2,16,4]{1,2,0:T(4,128)S(1)} copy-done((s32[2,16,4]{1,2,0:T(4,128)S(1)}, s32[2,16,4]{1,2,0:T(4,128)}, u32[]{:S(2)}) %copy-start.14) | copy-done | bytes 536
  10.1 1.4 %local_part.1 = (f32[6,2,4,256]{3,2,1,0:T(4,128)S(1)}, f32[6,2,4,256]{3,2,1,0:T(4,128)S(1)}, f32[2,48,128]{2,1,0:T(8,128)S(1)}, f32[6,2,4,256]{3,2,1,0:T(4,128)S...) custom-call(f32[6,2,4,256]{3,2,1,0:T(4,128)S(1)} %copy-done.11, ...), custom_call_target="tpu_custom_call" | custom-call | tf_op jit(solution)/shard_map/local_part/pallas_call | solution.py:350
  11.5 16.2 %all_gather.3.g = f32[16,48,128]{2,1,0:T(8,128)S(1)} all-gather(f32[2,48,128]{2,1,0:T(8,128)S(1)} %get-tuple-element.18), channel_id=1, replica_groups=mesh['circ'=8,'span'=4] {'circ'}, dimensions={0}, use_global_device_ids=true | all-gather | bytes 442368 | tf_op jit(solution)/shard_map/all_gather | solution.py:364
  27.8 0.0 copy-start.1
  27.8 0.0 copy-start.3
  27.8 0.0 copy-start.7
  27.8 0.0 copy-start.9
  27.8 1.5 %interface_part.1 = (f32[6,2,4,256]{3,2,1,0:T(4,128)S(1)}, f32[6,2,4,256]{3,2,1,0:T(4,128)S(1)}, f32[6,2,4,256]{3,2,1,0:T(4,128)S(1)}, f32[6,2,4,256]{3,2,1,0:T(...) custom-call(f32[16,48,128]{2,1,0:T(8,128)S(1)} %all_gather.3.g, ...), custom_call_target="tpu_custom_call" | custom-call | tf_op jit(solution)/shard_map/interface_part/pallas_call | solution.py:367
  29.2 3.4 %collective-permute-start = (bf16[21,16,128]{2,1,0:T(8,128)(2,1)S(1)}, bf16[21,16,128]{2,1,0:T(8,128)(2,1)S(1)}, u32[]{:S(2)}, u32[]{:S(2)}) collective-permute-start(bf16[21,16,128]{2,1,0:T(8,128)(2,1)S(1)} %get-tuple-element.26), channel_id=1, source_target_pairs={{0,1},{1,2},{2,3},{4,5},{5,6},{6,7},{8,9},{9,10},{10,11},{12,13},{... | collective-permute-start | bytes 258056 | tf_op jit(solution)/shard_map/ppermute | solution.py:381
  32.7 1.3 %collective-permute-start.1 = (bf16[21,16,128]{2,1,0:T(8,128)(2,1)S(1)}, bf16[21,16,128]{2,1,0:T(8,128)(2,1)S(1)}, u32[]{:S(2)}, u32[]{:S(2)}) collective-permute-start(bf16[21,16,128]{2,1,0:T(8,128)(2,1)S(1)} %get-tuple-element.27), channel_id=1, source_target_pairs={{1,0},{2,1},{3,2},{5,4},{6,5},{7,6},{9,8},{10,9},{11,10},{13,12},{... | collective-permute-start | bytes 258056 | tf_op jit(solution)/shard_map/ppermute | solution.py:382
  34.0 1.0 %collective-permute-done.low = bf16[21,16,128]{2,1,0:T(8,128)(2,1)S(1)} collective-permute-done((bf16[21,16,128]{2,1,0:T(8,128)(2,1)S(1)}, bf16[21,16,128]{2,1,0:T(8,128)(2,1)S(1)}, u32[]{:S(2)}, u32[]{:S(2)}) %collective-permute-start) | collective-permute-done | bytes 86048 | tf_op jit(solution)/shard_map/ppermute | solution.py:381
  34.9 4.1 %collective-permute-done.1.high = bf16[21,16,128]{2,1,0:T(8,128)(2,1)S(1)} collective-permute-done((bf16[21,16,128]{2,1,0:T(8,128)(2,1)S(1)}, bf16[21,16,128]{2,1,0:T(8,128)(2,1)S(1)}, u32[]{:S(2)}, u32[]{:S(2)}) %collective-permute-start.1) | collective-permute-done | bytes 86048 | tf_op jit(solution)/shard_map/ppermute | solution.py:382
  39.1 0.0 copy-done.1
  39.1 0.0 copy-done.3
  39.1 0.0 copy-done.7
  39.1 0.0 copy-done.9
  39.1 1.9 %final_part.1 = (f32[6,2,4,256]{3,2,1,0:T(4,128)}, f32[6,2,4,256]{3,2,1,0:T(4,128)}) custom-call(bf16[21,16,128]{2,1,0:T(8,128)(2,1)S(1)} %collective-permute-done.low, bf16[21,16,128]{2,1,0:T(8,128)(2,1)S(1)} %collective-permute-done.1.high, f32[6,2,4,256]{3,2,1,0:T(4,128)S(1)} %get-tuple-element.28.o_r, f32[6,2,4,256]{3,2,1,0:T(4,128)S(1)} %get-tuple-element.29.o_s, ...), custom_call_target="tpu_custom_call" | custom-call | tf_op jit(solution)/shard_map/final_part/pallas_call | solution.py:383
Async XLA Ops:
  0.6 0.7 %copy-start.15 = (s32[2,16]{1,0:T(2,128)S(1)}, s32[2,16]{1,0:T(2,128)}, u32[]{:S(2)}) copy-start(s32[2,16]{1,0:T(2,128)} %refs_10_.1) | copy-start | bytes 388
  1.3 0.9 %copy-start = (bf16[6,6,2,4,256]{4,3,2,1,0:T(4,128)(2,1)S(1)}, bf16[6,6,2,4,256]{4,3,2,1,0:T(4,128)(2,1)}, u32[]{:S(2)}) copy-start(bf16[6,6,2,4,256]{4,3,2,1,0:T(4,128)(2,1)} %jo_r.1) | copy-start | bytes 442372
  2.2 0.9 %copy-start.2 = (bf16[6,6,2,4,256]{4,3,2,1,0:T(4,128)(2,1)S(1)}, bf16[6,6,2,4,256]{4,3,2,1,0:T(4,128)(2,1)}, u32[]{:S(2)}) copy-start(bf16[6,6,2,4,256]{4,3,2,1,0:T(4,128)(2,1)} %jo_s.1) | copy-start | bytes 442372
  3.1 0.8 %copy-start.4 = (f32[6,2,4,256]{3,2,1,0:T(4,128)S(1)}, f32[6,2,4,256]{3,2,1,0:T(4,128)}, u32[]{:S(2)}) copy-start(f32[6,2,4,256]{3,2,1,0:T(4,128)} %jd_r.1) | copy-start | bytes 147460
  3.9 0.8 %copy-start.5 = (f32[6,2,4,256]{3,2,1,0:T(4,128)S(1)}, f32[6,2,4,256]{3,2,1,0:T(4,128)}, u32[]{:S(2)}) copy-start(f32[6,2,4,256]{3,2,1,0:T(4,128)} %jd_s.1) | copy-start | bytes 147460
  4.7 0.8 %copy-start.6 = (f32[6,2,4,256]{3,2,1,0:T(4,128)S(1)}, f32[6,2,4,256]{3,2,1,0:T(4,128)}, u32[]{:S(2)}) copy-start(f32[6,2,4,256]{3,2,1,0:T(4,128)} %src_r.1) | copy-start | bytes 147460
  5.5 0.8 %copy-start.8 = (f32[6,2,4,256]{3,2,1,0:T(4,128)S(1)}, f32[6,2,4,256]{3,2,1,0:T(4,128)}, u32[]{:S(2)}) copy-start(f32[6,2,4,256]{3,2,1,0:T(4,128)} %src_s.1) | copy-start | bytes 147460
  6.3 0.8 %copy-start.10 = (f32[2,16,4,128]{3,2,1,0:T(4,128)S(1)}, f32[2,16,4,128]{3,2,1,0:T(4,128)}, u32[]{:S(2)}) copy-start(f32[2,16,4,128]{3,2,1,0:T(4,128)} %refs_11_.1) | copy-start | bytes 196612
  7.2 0.8 %copy-start.11 = (f32[6,2,4,256]{3,2,1,0:T(4,128)S(1)}, f32[6,2,4,256]{3,2,1,0:T(4,128)}, u32[]{:S(2)}) copy-start(f32[6,2,4,256]{3,2,1,0:T(4,128)} %refs_0_.1) | copy-start | bytes 147460
  8.0 0.8 %copy-start.12 = (f32[6,2,4,256]{3,2,1,0:T(4,128)S(1)}, f32[6,2,4,256]{3,2,1,0:T(4,128)}, u32[]{:S(2)}) copy-start(f32[6,2,4,256]{3,2,1,0:T(4,128)} %refs_1_.1) | copy-start | bytes 147460
  8.8 0.7 %copy-start.13 = (bf16[6,2,256]{2,1,0:T(2,128)(2,1)S(1)}, bf16[6,2,256]{2,1,0:T(2,128)(2,1)}, u32[]{:S(2)}) copy-start(bf16[6,2,256]{2,1,0:T(2,128)(2,1)} %refs_8_.1) | copy-start | bytes 18436
  9.5 0.7 %copy-start.14 = (s32[2,16,4]{1,2,0:T(4,128)S(1)}, s32[2,16,4]{1,2,0:T(4,128)}, u32[]{:S(2)}) copy-start(s32[2,16,4]{1,2,0:T(4,128)} %param.21) | copy-start | bytes 1540
  27.8 11.3 %copy-start.1 = (bf16[6,6,2,4,256]{4,3,2,1,0:T(4,128)(2,1)S(1)}, bf16[6,6,2,4,256]{4,3,2,1,0:T(4,128)(2,1)}, u32[]{:S(2)}) copy-start(bf16[6,6,2,4,256]{4,3,2,1,0:T(4,128)(2,1)} %jo_r.1) | copy-start | bytes 442372
  27.8 11.3 %copy-start.3 = (bf16[6,6,2,4,256]{4,3,2,1,0:T(4,128)(2,1)S(1)}, bf16[6,6,2,4,256]{4,3,2,1,0:T(4,128)(2,1)}, u32[]{:S(2)}) copy-start(bf16[6,6,2,4,256]{4,3,2,1,0:T(4,128)(2,1)} %jo_s.1) | copy-start | bytes 442372
  27.8 11.3 %copy-start.7 = (f32[6,2,4,256]{3,2,1,0:T(4,128)S(1)}, f32[6,2,4,256]{3,2,1,0:T(4,128)}, u32[]{:S(2)}) copy-start(f32[6,2,4,256]{3,2,1,0:T(4,128)} %src_r.1) | copy-start | bytes 147460
  27.8 11.3 %copy-start.9 = (f32[6,2,4,256]{3,2,1,0:T(4,128)S(1)}, f32[6,2,4,256]{3,2,1,0:T(4,128)}, u32[]{:S(2)}) copy-start(f32[6,2,4,256]{3,2,1,0:T(4,128)} %src_s.1) | copy-start | bytes 147460
  29.2 5.7 %collective-permute-start = (bf16[21,16,128]{2,1,0:T(8,128)(2,1)S(1)}, bf16[21,16,128]{2,1,0:T(8,128)(2,1)S(1)}, u32[]{:S(2)}, u32[]{:S(2)}) collective-permute-start(bf16[21,16,128]{2,1,0:T(8,128)(2,1)S(1)} %get-tuple-element.26), channel_id=1, source_target_pairs={{0,1},{1,2},{2,3},{4,5},{5,6},{6,7},{8,9},{9,10},{10,11},{12,13},{... | collective-permute-start | bytes 258056 | tf_op jit(solution)/shard_map/ppermute | solution.py:381
  32.7 6.4 %collective-permute-start.1 = (bf16[21,16,128]{2,1,0:T(8,128)(2,1)S(1)}, bf16[21,16,128]{2,1,0:T(8,128)(2,1)S(1)}, u32[]{:S(2)}, u32[]{:S(2)}) collective-permute-start(bf16[21,16,128]{2,1,0:T(8,128)(2,1)S(1)} %get-tuple-element.27), channel_id=1, source_target_pairs={{1,0},{2,1},{3,2},{5,4},{6,5},{7,6},{9,8},{10,9},{11,10},{13,12},{... | collective-permute-start | bytes 258056 | tf_op jit(solution)/shard_map/ppermute | solution.py:382
where the time goes:
time: 41.6 us; the launch traced here: 41 us
  blocking collectives  16.2 us (39%)
  local copies, waits for them, and re-layouts  9.51 us (23%)
  waiting for transfers between devices  5.1 us (12%)
  Pallas kernels  4.74 us (11%)
  starting transfers between devices  4.69 us (11%)
  between operations  0.7 us (2%)
    all_gather x1, blocking collectives, per_device(): whole = lax.all_gather(share, 'circ', axis=0, tiled=True)  16.2 us
    unnamed x32, local copies, waits for them, and re-layouts  9.51 us
    ppermute x1, waiting for transfers between devices, per_device(): high = lax.ppermute(down, 'span', [(i + 1, i) for i in range(bands - 1)])  4.12 us
    ppermute x1, starting transfers between devices, per_device(): low = lax.ppermute(up, 'span', [(i, i + 1) for i in range(bands - 1)])  3.4 us
    pallas_call x1, Pallas kernels, per_device(): pl.pallas_call(third_kernel, out_shape=(field, field), in_specs=[vmem] *...  1.87 us
    pallas_call x1, Pallas kernels, per_device(): pl.pallas_call(second_kernel, out_shape=(field, field, field, field, list...  1.48 us
    pallas_call x1, Pallas kernels, per_device(): pl.pallas_call(first_kernel, out_shape=(field, field, jax.ShapeDtypeStruc...  1.39 us
    ppermute x1, starting transfers between devices, per_device(): high = lax.ppermute(down, 'span', [(i + 1, i) for i in range(bands - 1)])  1.29 us
  transfers between devices with their start and end apart: 2, of which 2 were waited for; matrix products, arithmetic and copies ran while one was open for 0% of the time, Pallas kernels for 0%

commit v1 on v0

--- a/solution.py
+++ b/solution.py
@@ -353,14 +353,14 @@
             field, field, jax.ShapeDtypeStruct((own_blocks, rows * 24, TILE), f32),
             shapes[0], shapes[1], shapes[11], shapes[9], shapes[10],
         ),
-        in_specs=[pl.BlockSpec(memory_space=pl.ANY)] * 12,
+        in_specs=[pl.BlockSpec(memory_space=pltpu.HBM)] * 12,
         out_specs=(vmem,) * 8,
         scratch_shapes=[pltpu.VMEM(x.shape, x.dtype) for x in shapes[2:9]]
         + [padded] * 4
         + [pltpu.SemaphoreType.DMA((12,))],
         compiler_params=params,
         name="local_part",
-    )(*arguments)
+    )(*[pltpu.with_memory_space_constraint(x, pltpu.HBM) for x in arguments])
     whole = lax.all_gather(share, "circ", axis=0, tiled=True)
     tiles = jax.ShapeDtypeStruct((total // 2 + var_count * own_blocks + 1, 16, TILE), jnp.bfloat16)
     listed = jax.ShapeDtypeStruct((rows, spread - 2 + own_blocks, 8, TILE), f32)

time: 41.6 us -> 31.9 us (0.77); the launches traced: 41 us -> 31.7 us
  local copies, waits for them, and re-layouts: 9.51 us -> 0.02 us
    unnamed x32 -> x12, local copies, waits for them, and re-layouts: 9.51 us -> 0.02 us
where the time goes in v1:
time: 31.9 us; the launch traced here: 31.7 us
  blocking collectives  16.2 us (51%)
  waiting for transfers between devices  5.1 us (16%)
  Pallas kernels  4.97 us (16%)
  starting transfers between devices  4.69 us (15%)
  between operations  0.71 us (2%)
    all_gather x1, blocking collectives, per_device(): whole = lax.all_gather(share, 'circ', axis=0, tiled=True)  16.2 us
    ppermute x1, waiting for transfers between devices, per_device(): high = lax.ppermute(down, 'span', [(i + 1, i) for i in range(bands - 1)])  4.12 us
    ppermute x1, starting transfers between devices, per_device(): low = lax.ppermute(up, 'span', [(i, i + 1) for i in range(bands - 1)])  3.4 us
    pallas_call x1, Pallas kernels, per_device(): pl.pallas_call(third_kernel, out_shape=(field, field), in_specs=[vmem] *...  1.87 us
    pallas_call x1, Pallas kernels, per_device(): pl.pallas_call(first_kernel, out_shape=(field, field, jax.ShapeDtypeStruc...  1.62 us
    pallas_call x1, Pallas kernels, per_device(): pl.pallas_call(second_kernel, out_shape=(field, field, field, field, list...  1.49 us
    ppermute x1, starting transfers between devices, per_device(): high = lax.ppermute(down, 'span', [(i + 1, i) for i in range(bands - 1)])  1.29 us
    ppermute x1, waiting for transfers between devices, per_device(): low = lax.ppermute(up, 'span', [(i, i + 1) for i in range(bands - 1)])  0.98 us
  transfers between devices with their start and end apart: 2, of which 2 were waited for; matrix products, arithmetic and copies ran while one was open for 0% of the time, Pallas kernels for 0%

profile of v1, /device:TPU:0, one launch (start us, length us, event | category | flops | bytes accessed | tf_op | source)
XLA Modules:
  0.0 31.7 jit_solution(16198724564198142983)
XLA Ops:
  0.6 1.6 %local_part.1 = (f32[6,2,4,256]{3,2,1,0:T(4,128)S(1)}, f32[6,2,4,256]{3,2,1,0:T(4,128)S(1)}, f32[2,48,128]{2,1,0:T(8,128)S(1)}, f32[6,2,4,256]{3,2,1,0:T(4,128)S...) custom-call(f32[6,2,4,256]{3,2,1,0:T(4,128)} %refs_0_.1, ...), custom_call_target="tpu_custom_call" | custom-call | tf_op jit(solution)/shard_map/local_part/pallas_call | solution.py:350
  2.3 16.2 %all_gather.3.g = f32[16,48,128]{2,1,0:T(8,128)S(1)} all-gather(f32[2,48,128]{2,1,0:T(8,128)S(1)} %get-tuple-element.18), channel_id=1, replica_groups=mesh['circ'=8,'span'=4] {'circ'}, dimensions={0}, use_global_device_ids=true | all-gather | bytes 442368 | tf_op jit(solution)/shard_map/all_gather | solution.py:364
  18.5 0.0 copy-start
  18.5 0.0 copy-start.1
  18.5 0.0 copy-start.2
  18.5 0.0 copy-start.3
  18.5 0.0 copy-start.4
  18.5 0.0 copy-start.5
  18.5 1.5 %interface_part.1 = (f32[6,2,4,256]{3,2,1,0:T(4,128)S(1)}, f32[6,2,4,256]{3,2,1,0:T(4,128)S(1)}, f32[6,2,4,256]{3,2,1,0:T(4,128)S(1)}, f32[6,2,4,256]{3,2,1,0:T(...) custom-call(f32[16,48,128]{2,1,0:T(8,128)S(1)} %all_gather.3.g, ...), custom_call_target="tpu_custom_call" | custom-call | tf_op jit(solution)/shard_map/interface_part/pallas_call | solution.py:367
  20.0 3.4 %collective-permute-start = (bf16[21,16,128]{2,1,0:T(8,128)(2,1)S(1)}, bf16[21,16,128]{2,1,0:T(8,128)(2,1)S(1)}, u32[]{:S(2)}, u32[]{:S(2)}) collective-permute-start(bf16[21,16,128]{2,1,0:T(8,128)(2,1)S(1)} %get-tuple-element.26), channel_id=1, source_target_pairs={{0,1},{1,2},{2,3},{4,5},{5,6},{6,7},{8,9},{9,10},{10,11},{12,13},{... | collective-permute-start | bytes 258056 | tf_op jit(solution)/shard_map/ppermute | solution.py:381
  23.4 1.3 %collective-permute-start.1 = (bf16[21,16,128]{2,1,0:T(8,128)(2,1)S(1)}, bf16[21,16,128]{2,1,0:T(8,128)(2,1)S(1)}, u32[]{:S(2)}, u32[]{:S(2)}) collective-permute-start(bf16[21,16,128]{2,1,0:T(8,128)(2,1)S(1)} %get-tuple-element.27), channel_id=1, source_target_pairs={{1,0},{2,1},{3,2},{5,4},{6,5},{7,6},{9,8},{10,9},{11,10},{13,12},{... | collective-permute-start | bytes 258056 | tf_op jit(solution)/shard_map/ppermute | solution.py:382
  24.7 1.0 %collective-permute-done.low = bf16[21,16,128]{2,1,0:T(8,128)(2,1)S(1)} collective-permute-done((bf16[21,16,128]{2,1,0:T(8,128)(2,1)S(1)}, bf16[21,16,128]{2,1,0:T(8,128)(2,1)S(1)}, u32[]{:S(2)}, u32[]{:S(2)}) %collective-permute-start) | collective-permute-done | bytes 86048 | tf_op jit(solution)/shard_map/ppermute | solution.py:381
  25.7 4.1 %collective-permute-done.1.high = bf16[21,16,128]{2,1,0:T(8,128)(2,1)S(1)} collective-permute-done((bf16[21,16,128]{2,1,0:T(8,128)(2,1)S(1)}, bf16[21,16,128]{2,1,0:T(8,128)(2,1)S(1)}, u32[]{:S(2)}, u32[]{:S(2)}) %collective-permute-start.1) | collective-permute-done | bytes 86048 | tf_op jit(solution)/shard_map/ppermute | solution.py:382
  29.8 0.0 copy-done
  29.8 0.0 copy-done.1
  29.8 0.0 copy-done.2
  29.8 0.0 copy-done.3
  29.8 0.0 copy-done.4
  29.8 0.0 copy-done.5
  29.8 1.9 %final_part.1 = (f32[6,2,4,256]{3,2,1,0:T(4,128)}, f32[6,2,4,256]{3,2,1,0:T(4,128)}) custom-call(bf16[21,16,128]{2,1,0:T(8,128)(2,1)S(1)} %collective-permute-done.low, bf16[21,16,128]{2,1,0:T(8,128)(2,1)S(1)} %collective-permute-done.1.high, f32[6,2,4,256]{3,2,1,0:T(4,128)S(1)} %get-tuple-element.28.o_r, f32[6,2,4,256]{3,2,1,0:T(4,128)S(1)} %get-tuple-element.29.o_s, ...), custom_call_target="tpu_custom_call" | custom-call | tf_op jit(solution)/shard_map/final_part/pallas_call | solution.py:383
Async XLA Ops:
  18.5 11.3 %copy-start = (bf16[6,6,2,4,256]{4,3,2,1,0:T(4,128)(2,1)S(1)}, bf16[6,6,2,4,256]{4,3,2,1,0:T(4,128)(2,1)}, u32[]{:S(2)}) copy-start(bf16[6,6,2,4,256]{4,3,2,1,0:T(4,128)(2,1)} %jo_r.1) | copy-start | bytes 442372
  18.5 11.3 %copy-start.1 = (bf16[6,6,2,4,256]{4,3,2,1,0:T(4,128)(2,1)S(1)}, bf16[6,6,2,4,256]{4,3,2,1,0:T(4,128)(2,1)}, u32[]{:S(2)}) copy-start(bf16[6,6,2,4,256]{4,3,2,1,0:T(4,128)(2,1)} %jo_s.1) | copy-start | bytes 442372
  18.5 11.3 %copy-start.2 = (f32[6,2,4,256]{3,2,1,0:T(4,128)S(1)}, f32[6,2,4,256]{3,2,1,0:T(4,128)}, u32[]{:S(2)}) copy-start(f32[6,2,4,256]{3,2,1,0:T(4,128)} %jd_r.1) | copy-start | bytes 147460
  18.5 11.3 %copy-start.3 = (f32[6,2,4,256]{3,2,1,0:T(4,128)S(1)}, f32[6,2,4,256]{3,2,1,0:T(4,128)}, u32[]{:S(2)}) copy-start(f32[6,2,4,256]{3,2,1,0:T(4,128)} %jd_s.1) | copy-start | bytes 147460
  18.5 11.3 %copy-start.4 = (f32[6,2,4,256]{3,2,1,0:T(4,128)S(1)}, f32[6,2,4,256]{3,2,1,0:T(4,128)}, u32[]{:S(2)}) copy-start(f32[6,2,4,256]{3,2,1,0:T(4,128)} %src_r.1) | copy-start | bytes 147460
  18.5 11.3 %copy-start.5 = (f32[6,2,4,256]{3,2,1,0:T(4,128)S(1)}, f32[6,2,4,256]{3,2,1,0:T(4,128)}, u32[]{:S(2)}) copy-start(f32[6,2,4,256]{3,2,1,0:T(4,128)} %src_s.1) | copy-start | bytes 147460
  20.0 5.7 %collective-permute-start = (bf16[21,16,128]{2,1,0:T(8,128)(2,1)S(1)}, bf16[21,16,128]{2,1,0:T(8,128)(2,1)S(1)}, u32[]{:S(2)}, u32[]{:S(2)}) collective-permute-start(bf16[21,16,128]{2,1,0:T(8,128)(2,1)S(1)} %get-tuple-element.26), channel_id=1, source_target_pairs={{0,1},{1,2},{2,3},{4,5},{5,6},{6,7},{8,9},{9,10},{10,11},{12,13},{... | collective-permute-start | bytes 258056 | tf_op jit(solution)/shard_map/ppermute | solution.py:381
  23.4 6.4 %collective-permute-start.1 = (bf16[21,16,128]{2,1,0:T(8,128)(2,1)S(1)}, bf16[21,16,128]{2,1,0:T(8,128)(2,1)S(1)}, u32[]{:S(2)}, u32[]{:S(2)}) collective-permute-start(bf16[21,16,128]{2,1,0:T(8,128)(2,1)S(1)} %get-tuple-element.27), channel_id=1, source_target_pairs={{1,0},{2,1},{3,2},{5,4},{6,5},{7,6},{9,8},{10,9},{11,10},{13,12},{... | collective-permute-start | bytes 258056 | tf_op jit(solution)/shard_map/ppermute | solution.py:382

commit v2 on v1

--- a/solution.py
+++ b/solution.py
@@ -125,8 +125,8 @@
 
 
 def second_kernel(
-    g, v_r, v_s, a_r, a_s, weights, margin, count,
-    o_r, o_s, h_r, h_s, q_out, p_out, up, down, flux, held, spot,
+    mine, other, v_r, v_s, a_r, a_s, weights, margin, count,
+    o_r, o_s, h_r, h_s, q_out, p_out, up, down, flux, held, spot, g,
 ):
     var_count, rows, layers, cells = a_r.shape
     total = g.shape[0]
@@ -142,6 +142,11 @@
     left = wrapped(first_block - 1 + total, total)
     right = wrapped(first_block + own_blocks, total)
 
+    core = jnp.bitwise_and(lax.axis_index("circ"), 1)
+    for chip in range(total // own_blocks // 2):
+        for i in range(own_blocks):
+            g[(2 * chip + core) * own_blocks + i] = mine[chip * own_blocks + i]
+            g[(2 * chip + 1 - core) * own_blocks + i] = other[chip * own_blocks + i]
     spot[0:2, :] = g[left, 6:8, :]
     spot[2:4, :] = g[left, 14:16, :]
     spot[4:6, :] = g[right, 6:8, :]
@@ -361,22 +366,27 @@
         compiler_params=params,
         name="local_part",
     )(*[pltpu.with_memory_space_constraint(x, pltpu.HBM) for x in arguments])
-    whole = lax.all_gather(share, "circ", axis=0, tiled=True)
+    members = lax.axis_size("circ")
+    cores = 2
+    alike = [list(range(core, members, cores)) for core in range(cores)]
+    mine = lax.all_gather(share, "circ", axis=0, tiled=True, axis_index_groups=alike)
+    other = lax.ppermute(mine, "circ", [(i, i ^ 1) for i in range(members)])
     tiles = jax.ShapeDtypeStruct((total // 2 + var_count * own_blocks + 1, 16, TILE), jnp.bfloat16)
     listed = jax.ShapeDtypeStruct((rows, spread - 2 + own_blocks, 8, TILE), f32)
     o_r, o_s, h_r, h_s, q, p, up, down = pl.pallas_call(
         second_kernel,
         out_shape=(field, field, field, field, listed, listed, tiles, tiles),
-        in_specs=[vmem] * 6 + [smem] * 2,
+        in_specs=[vmem] * 7 + [smem] * 2,
         out_specs=(vmem,) * 8,
         scratch_shapes=[
             pltpu.VMEM((rows, spread, 8, TILE), f32),
             pltpu.VMEM((var_count, 4 * layers, cells), f32),
             pltpu.VMEM((8, TILE), f32),
+            pltpu.VMEM((total, rows * 24, TILE), f32),
         ],
         compiler_params=params,
         name="interface_part",
-    )(whole, v_r, v_s, a_r, a_s, weights, margin, count)
+    )(mine, other, v_r, v_s, a_r, a_s, weights, margin, count)
     bands = lax.axis_size("span")
     low = lax.ppermute(up, "span", [(i, i + 1) for i in range(bands - 1)])
     high = lax.ppermute(down, "span", [(i + 1, i) for i in range(bands - 1)])

time: 31.9 us -> 32.6 us (1.022)
  waiting for transfers between devices: 5.1 us -> 6.52 us
  blocking collectives: 16.2 us -> 15.5 us
    ppermute x0 -> x1, waiting for transfers between devices: none -> 1.44 us  [per_device(): other = lax.ppermute(mine, 'circ', [(i, i ^ 1) for i in range(members)])]
    all_gather x1, blocking collectives: 16.2 us -> 15.5 us  [per_device(): lax.all_gather(share, 'circ', axis=0, tiled=True, axis_index_groups=alike)]
  transfers between devices with their start and end apart: 2 -> 3, of which waited for: 2 -> 3; matrix products, arithmetic and copies ran while one was open for 0% -> 0% of each run, Pallas kernels for 0% -> 0%
where the time goes in v2:
time: 32.6 us; the launch traced here: 32.4 us
  blocking collectives  15.5 us (48%)
  waiting for transfers between devices  6.52 us (20%)
  Pallas kernels  5.01 us (15%)
  starting transfers between devices  4.69 us (14%)
  between operations  0.71 us (2%)
    all_gather x1, blocking collectives, per_device(): lax.all_gather(share, 'circ', axis=0, tiled=True, axis_index_groups=alike)  15.5 us
    ppermute x1, waiting for transfers between devices, per_device(): high = lax.ppermute(down, 'span', [(i + 1, i) for i in range(bands - 1)])  4.3 us
    ppermute x1, starting transfers between devices, per_device(): low = lax.ppermute(up, 'span', [(i, i + 1) for i in range(bands - 1)])  3.4 us
    pallas_call x1, Pallas kernels, per_device(): pl.pallas_call(third_kernel, out_shape=(field, field), in_specs=[vmem] *...  1.88 us
    pallas_call x1, Pallas kernels, per_device(): pl.pallas_call(first_kernel, out_shape=(field, field, jax.ShapeDtypeStruc...  1.62 us
    pallas_call x1, Pallas kernels, per_device(): pl.pallas_call(second_kernel, out_shape=(field, field, field, field, list...  1.51 us
    ppermute x1, waiting for transfers between devices, per_device(): other = lax.ppermute(mine, 'circ', [(i, i ^ 1) for i in range(members)])  1.44 us
    ppermute x1, starting transfers between devices, per_device(): high = lax.ppermute(down, 'span', [(i + 1, i) for i in range(bands - 1)])  1.29 us
  transfers between devices with their start and end apart: 3, of which 3 were waited for; matrix products, arithmetic and copies ran while one was open for 0% of the time, Pallas kernels for 0%

profile of v2, /device:TPU:0, one launch (start us, length us, event | category | flops | bytes accessed | tf_op | source)
XLA Modules:
  0.0 32.4 jit_solution(10507388662451687194)
XLA Ops:
  0.6 1.6 %local_part.1 = (f32[6,2,4,256]{3,2,1,0:T(4,128)S(1)}, f32[6,2,4,256]{3,2,1,0:T(4,128)S(1)}, f32[2,48,128]{2,1,0:T(8,128)S(1)}, f32[6,2,4,256]{3,2,1,0:T(4,128)S...) custom-call(f32[6,2,4,256]{3,2,1,0:T(4,128)} %refs_0_.1, ...), custom_call_target="tpu_custom_call" | custom-call | tf_op jit(solution)/shard_map/local_part/pallas_call | solution.py:355
  2.3 15.5 %all_gather.3.mine = f32[8,48,128]{2,1,0:T(8,128)S(1)} all-gather(f32[2,48,128]{2,1,0:T(8,128)S(1)} %get-tuple-element.18), channel_id=1, replica_groups={{0,8,16,24},{4,12,20,28},{1,9,17,25},{5,13,21,29},{2,10,18,26},{6,14,22..., dimensions={0}, use_global_device_ids=true | all-gather | bytes 245760 | tf_op jit(solution)/shard_map/all_gather | solution.py:372
  17.7 0.0 collective-permute-start
  17.7 1.4 %collective-permute-done.other = f32[8,48,128]{2,1,0:T(8,128)S(1)} collective-permute-done((f32[8,48,128]{2,1,0:T(8,128)S(1)}, f32[8,48,128]{2,1,0:T(8,128)S(1)}, u32[]{:S(2)}, u32[]{:S(2)}) %collective-permute-start) | collective-permute-done | bytes 196640 | tf_op jit(solution)/shard_map/ppermute | solution.py:373
  19.2 0.0 copy-start
  19.2 0.0 copy-start.1
  19.2 0.0 copy-start.2
  19.2 0.0 copy-start.3
  19.2 0.0 copy-start.4
  19.2 0.0 copy-start.5
  19.2 1.5 %interface_part.1 = (f32[6,2,4,256]{3,2,1,0:T(4,128)S(1)}, f32[6,2,4,256]{3,2,1,0:T(4,128)S(1)}, f32[6,2,4,256]{3,2,1,0:T(4,128)S(1)}, f32[6,2,4,256]{3,2,1,0:T(...) custom-call(f32[8,48,128]{2,1,0:T(8,128)S(1)} %all_gather.3.mine, ...), custom_call_target="tpu_custom_call" | custom-call | tf_op jit(solution)/shard_map/interface_part/pallas_call | solution.py:376
  20.7 3.4 %collective-permute-start.1 = (bf16[21,16,128]{2,1,0:T(8,128)(2,1)S(1)}, bf16[21,16,128]{2,1,0:T(8,128)(2,1)S(1)}, u32[]{:S(2)}, u32[]{:S(2)}) collective-permute-start(bf16[21,16,128]{2,1,0:T(8,128)(2,1)S(1)} %get-tuple-element.26), channel_id=1, source_target_pairs={{0,1},{1,2},{2,3},{4,5},{5,6},{6,7},{8,9},{9,10},{10,11},{12,13},{... | collective-permute-start | bytes 258056 | tf_op jit(solution)/shard_map/ppermute | solution.py:391
  24.1 1.3 %collective-permute-start.2 = (bf16[21,16,128]{2,1,0:T(8,128)(2,1)S(1)}, bf16[21,16,128]{2,1,0:T(8,128)(2,1)S(1)}, u32[]{:S(2)}, u32[]{:S(2)}) collective-permute-start(bf16[21,16,128]{2,1,0:T(8,128)(2,1)S(1)} %get-tuple-element.27), channel_id=1, source_target_pairs={{1,0},{2,1},{3,2},{5,4},{6,5},{7,6},{9,8},{10,9},{11,10},{13,12},{... | collective-permute-start | bytes 258056 | tf_op jit(solution)/shard_map/ppermute | solution.py:392
  25.4 0.8 %collective-permute-done.1.low = bf16[21,16,128]{2,1,0:T(8,128)(2,1)S(1)} collective-permute-done((bf16[21,16,128]{2,1,0:T(8,128)(2,1)S(1)}, bf16[21,16,128]{2,1,0:T(8,128)(2,1)S(1)}, u32[]{:S(2)}, u32[]{:S(2)}) %collective-permute-start.1) | collective-permute-done | bytes 86048 | tf_op jit(solution)/shard_map/ppermute | solution.py:391
  26.2 4.3 %collective-permute-done.2.high = bf16[21,16,128]{2,1,0:T(8,128)(2,1)S(1)} collective-permute-done((bf16[21,16,128]{2,1,0:T(8,128)(2,1)S(1)}, bf16[21,16,128]{2,1,0:T(8,128)(2,1)S(1)}, u32[]{:S(2)}, u32[]{:S(2)}) %collective-permute-start.2) | collective-permute-done | bytes 86048 | tf_op jit(solution)/shard_map/ppermute | solution.py:392
  30.5 0.0 copy-done
  30.5 0.0 copy-done.1
  30.5 0.0 copy-done.2
  30.5 0.0 copy-done.3
  30.5 0.0 copy-done.4
  30.5 0.0 copy-done.5
  30.5 1.9 %final_part.1 = (f32[6,2,4,256]{3,2,1,0:T(4,128)}, f32[6,2,4,256]{3,2,1,0:T(4,128)}) custom-call(bf16[21,16,128]{2,1,0:T(8,128)(2,1)S(1)} %collective-permute-done.1.low, bf16[21,16,128]{2,1,0:T(8,128)(2,1)S(1)} %collective-permute-done.2.high, f32[6,2,4,256]{3,2,1,0:T(4,128)S(1)} %get-tuple-element.28.o_r, f32[6,2,4,256]{3,2,1,0:T(4,128)S(1)} %get-tuple-element.29.o_s, ...), custom_call_target="tpu_custom_call" | custom-call | tf_op jit(solution)/shard_map/final_part/pallas_call | solution.py:393
Async XLA Ops:
  17.7 1.4 %collective-permute-start = (f32[8,48,128]{2,1,0:T(8,128)S(1)}, f32[8,48,128]{2,1,0:T(8,128)S(1)}, u32[]{:S(2)}, u32[]{:S(2)}) collective-permute-start(f32[8,48,128]{2,1,0:T(8,128)S(1)} %all_gather.3.mine), channel_id=1, source_target_pairs={{0,4},{4,0},{8,12},{12,8},{16,20},{20,16},{24,28},{28,24},{1,5},{5... | collective-permute-start | bytes 589832 | tf_op jit(solution)/shard_map/ppermute | solution.py:373
  19.2 11.3 %copy-start = (bf16[6,6,2,4,256]{4,3,2,1,0:T(4,128)(2,1)S(1)}, bf16[6,6,2,4,256]{4,3,2,1,0:T(4,128)(2,1)}, u32[]{:S(2)}) copy-start(bf16[6,6,2,4,256]{4,3,2,1,0:T(4,128)(2,1)} %jo_r.1) | copy-start | bytes 442372
  19.2 11.3 %copy-start.1 = (bf16[6,6,2,4,256]{4,3,2,1,0:T(4,128)(2,1)S(1)}, bf16[6,6,2,4,256]{4,3,2,1,0:T(4,128)(2,1)}, u32[]{:S(2)}) copy-start(bf16[6,6,2,4,256]{4,3,2,1,0:T(4,128)(2,1)} %jo_s.1) | copy-start | bytes 442372
  19.2 11.3 %copy-start.2 = (f32[6,2,4,256]{3,2,1,0:T(4,128)S(1)}, f32[6,2,4,256]{3,2,1,0:T(4,128)}, u32[]{:S(2)}) copy-start(f32[6,2,4,256]{3,2,1,0:T(4,128)} %jd_r.1) | copy-start | bytes 147460
  19.2 11.3 %copy-start.3 = (f32[6,2,4,256]{3,2,1,0:T(4,128)S(1)}, f32[6,2,4,256]{3,2,1,0:T(4,128)}, u32[]{:S(2)}) copy-start(f32[6,2,4,256]{3,2,1,0:T(4,128)} %jd_s.1) | copy-start | bytes 147460
  19.2 11.4 %copy-start.4 = (f32[6,2,4,256]{3,2,1,0:T(4,128)S(1)}, f32[6,2,4,256]{3,2,1,0:T(4,128)}, u32[]{:S(2)}) copy-start(f32[6,2,4,256]{3,2,1,0:T(4,128)} %src_r.1) | copy-start | bytes 147460
  19.2 11.4 %copy-start.5 = (f32[6,2,4,256]{3,2,1,0:T(4,128)S(1)}, f32[6,2,4,256]{3,2,1,0:T(4,128)}, u32[]{:S(2)}) copy-start(f32[6,2,4,256]{3,2,1,0:T(4,128)} %src_s.1) | copy-start | bytes 147460
  20.7 5.5 %collective-permute-start.1 = (bf16[21,16,128]{2,1,0:T(8,128)(2,1)S(1)}, bf16[21,16,128]{2,1,0:T(8,128)(2,1)S(1)}, u32[]{:S(2)}, u32[]{:S(2)}) collective-permute-start(bf16[21,16,128]{2,1,0:T(8,128)(2,1)S(1)} %get-tuple-element.26), channel_id=1, source_target_pairs={{0,1},{1,2},{2,3},{4,5},{5,6},{6,7},{8,9},{9,10},{10,11},{12,13},{... | collective-permute-start | bytes 258056 | tf_op jit(solution)/shard_map/ppermute | solution.py:391
  24.1 6.4 %collective-permute-start.2 = (bf16[21,16,128]{2,1,0:T(8,128)(2,1)S(1)}, bf16[21,16,128]{2,1,0:T(8,128)(2,1)S(1)}, u32[]{:S(2)}, u32[]{:S(2)}) collective-permute-start(bf16[21,16,128]{2,1,0:T(8,128)(2,1)S(1)} %get-tuple-element.27), channel_id=1, source_target_pairs={{1,0},{2,1},{3,2},{5,4},{6,5},{7,6},{9,8},{10,9},{11,10},{13,12},{... | collective-permute-start | bytes 258056 | tf_op jit(solution)/shard_map/ppermute | solution.py:392
